TPU v7x, 32 devices: a whole 2x2x4 slice. The times are simulated.
32 devices in a mesh: groups: 2 (over y), mp: 8 (over z, x), hidden: 2 (over core).
Axes of the slice: x: 2, y: 2, z: 4, core: 2. Of those that a mesh axis runs over, the one named last changes fastest.
Arguments:
- tokens: bfloat16 [48, 8192], P(('groups', 'mp'), 'hidden'), parts along dimension 0, may hold values from -6 to 6
- gate_weight: bfloat16 [8192, 2, 13312], P('hidden', None, 'mp'), may hold values from -0.0625 to 0.0625
- up_weight: bfloat16 [8192, 2, 13312], P('hidden', None, 'mp'), may hold values from -0.0625 to 0.0625
- down_weight: bfloat16 [2, 13312, 8192], P('hidden', None, 'mp'), may hold values from -0.0390625 to 0.0390625
Outputs:
- mixed: bfloat16 [48, 8192], P(('groups', 'hidden'), 'mp'), parts along dimension 0
There are 2 independent parts, one for each index of `groups`. A program takes and returns all parts, laid end to end along the dimension named above; an argument that names none is the same for every part. Nothing has to cross between parts.
All inputs are finite; a program needn't handle non-finite values.
Results may differ from a plain program's by a relative error of at most 0.0049.
Values may be sent and summed in bfloat16 or wider, within the bound.
A program may use at most 192 MiB of HBM per device.

v0:
```python
import jax
import jax.numpy as jnp
from jax import lax
from jax.sharding import PartitionSpec as P


def projector(gate_part, up_part, piece):
    gate = jnp.einsum("td,dbf->tbf", piece, gate_part, preferred_element_type=jnp.float32)
    up = jnp.einsum("td,dbf->tbf", piece, up_part, preferred_element_type=jnp.float32)
    return jnp.stack([gate, up])


def down_adder(weights, piece):
    return jnp.einsum("tbn,bnd->td", piece, weights, preferred_element_type=jnp.float32)


def shards(tokens, gate_weight, up_weight, down_weight):
    partial_sums = projector(
        gate_weight, up_weight, lax.all_gather(tokens, "mp", axis=0, tiled=True)
    )
    summed = lax.psum_scatter(partial_sums, "hidden", scatter_dimension=2, tiled=True)
    activation = (jax.nn.silu(summed[0]) * summed[1]).astype(jnp.bfloat16)
    partial_out = down_adder(down_weight, lax.all_gather(activation, "mp", axis=2, tiled=True))
    mixed = lax.psum_scatter(partial_out, "hidden", scatter_dimension=0, tiled=True)
    return mixed.astype(jnp.bfloat16)


def solution(mesh):
    in_specs = (
        P(("groups", "mp"), "hidden"),
        P("hidden", None, "mp"),
        P("hidden", None, "mp"),
        P("hidden", None, "mp"),
    )
    out_specs = P(("groups", "hidden"), "mp")
    return jax.shard_map(shards, mesh=mesh, in_specs=in_specs, out_specs=out_specs, check_vma=False)
```

profile of v0, /device:TPU:0, one launch (start us, length us, event | category | flops | bytes accessed | tf_op | source)
XLA Modules:
  0.0 150.1 jit_solution(12179379353571300341)
XLA Ops:
  6.5 0.0 all-reduce.5.cloned.1.call-start
  6.5 32.7 %all-gather = bf16[8,3,4096]{2,1,0:T(4,128)(2,1)S(1)} all-gather(bf16[1,3,4096]{2,1,0:T(4,128)(2,1)} %bitcast.30), channel_id=1, replica_groups=mesh['groups'=2,'mp'=8,'hidden'=2] {'mp'}, dimensions={0}, use_global_device_ids=true | all-gather | bytes 221184 | tf_op jit(solution)/shard_map/all_gather | solution.py:19
  39.3 0.2 reshape.62
  39.4 15.7 %fusion.10 = f32[1,24,2,1664]{3,1,2,0:T(8,128)S(1)} fusion(bf16[24,4096,1]{1,0,2:T(8,128)(2,1)S(1)} %reshape.62, bf16[4096,2,1664]{2,1,0:T(2,128)(2,1)} %param.6), kind=kOutput, calls=%fused_computation.7 | convolution fusion | flops 654311424 | bytes 27779072 | tf_op jit(solution)/shard_map/td,dbf->tbf/dot_general | solution.py:9
  55.2 0.0 copy-start
  55.2 15.7 %fusion.7 = f32[1,24,2,1664]{3,1,2,0:T(8,128)S(1)} fusion(bf16[24,4096,1]{1,0,2:T(8,128)(2,1)S(1)} %reshape.62, bf16[4096,2,1664]{2,1,0:T(2,128)(2,1)} %param.5), kind=kOutput, calls=%fused_computation.6 | convolution fusion | flops 654311424 | bytes 27779072 | tf_op jit(solution)/shard_map/td,dbf->tbf/dot_general | solution.py:8
  70.9 0.9 pad_maximum_fusion
  71.8 0.0 all-reduce.5.cloned.1.call-update
  71.9 0.0 copy-done
  71.9 0.7 fusion.16
  72.5 19.4 %all-reduce.5.cloned.1.call-done = f32[2,24,2,1664]{3,1,2,0:T(8,128)} async-done(((f32[2,24,2,1664]{3,1,2,0:T(8,128)}), f32[2,24,2,1664]{3,1,2,0:T(8,128)}) %all-reduce.5.cloned.1.call-update) | async-done | bytes 638992
  91.9 1.7 %fusion.15 = bf16[24,1,1664]{2,0,1:T(8,128)(2,1)S(1)} fusion(f32[2,24,2,1664]{3,1,2,0:T(8,128)} %all-reduce.5.cloned.1.call-done, u32[]{:T(128)S(6)} %convert, u32[]{:T(128)} %bitcast.11), kind=kLoop, calls=%fused_computation.12 | loop fusion | flops 239616 | bytes 399368 | tf_op jit(solution)/shard_map/convert_element_type | solution.py:22
  93.6 32.1 %all_gather.7 = bf16[24,1,13312]{2,0,1:T(8,128)(2,1)S(1)} all-gather(bf16[24,1,1664]{2,0,1:T(8,128)(2,1)S(1)} %fusion.15), channel_id=1, replica_groups=mesh['groups'=2,'mp'=8,'hidden'=2] {'mp'}, dimensions={2}, use_global_device_ids=true | all-gather | bytes 718848 | tf_op jit(solution)/shard_map/all_gather | solution.py:23
  125.7 10.7 %fusion.1 = f32[24,1024]{1,0:T(8,128)S(1)} fusion(bf16[1,13312,1024]{2,1,0:T(8,128)(2,1)} %param.7, bf16[24,1,13312]{2,0,1:T(8,128)(2,1)S(1)} %all_gather.7), kind=kOutput, calls=%fused_computation | convolution fusion | flops 654311424 | bytes 28000256 | tf_op jit(solution)/shard_map/tbn,bnd->td/dot_general | solution.py:14
  136.3 3.0 %fusion = f32[16,1024]{1,0:T(8,128)S(1)} fusion(f32[24,1024]{1,0:T(8,128)S(1)} %fusion.1), kind=kCustom, calls=%all-reduce-scatter | all-reduce-scatter fusion | flops 32769 | bytes 164352
  139.3 2.3 %collective-permute-start = (bf16[4,1024]{1,0:T(4,128)(2,1)S(1)}, bf16[4,1024]{1,0:T(4,128)(2,1)S(1)}, u32[]{:S(2)}, u32[]{:S(2)}) collective-permute-start(bf16[4,1024]{1,0:T(4,128)(2,1)S(1)} %slice.8), channel_id=1, source_target_pairs={{0,1},{2,3},{4,5},{6,7},{8,9},{10,11},{12,13},{14,15},{16,17},{18,... | collective-permute-start | bytes 24584
  142.2 0.2 collective-permute-done
  142.4 0.2 concatenate
  142.6 0.6 dynamic-slice_convert_fusion
  (1 shorter events, 0.0 us)
Async XLA Ops:
  6.5 85.4 %all-reduce.5.cloned.1.call-start = ((), (), s32[]{:S(2)}) async-start(), calls=%async_computation | async-start | bytes 1277952
  55.2 16.7 %copy-start = (u32[32]{0:T(128)S(1)}, u32[32]{0:T(128)}, u32[]{:S(2)}) copy-start(u32[32]{0:T(128)} %constant.7) | copy-start | bytes 388
  139.3 3.1 %collective-permute-start = (bf16[4,1024]{1,0:T(4,128)(2,1)S(1)}, bf16[4,1024]{1,0:T(4,128)(2,1)S(1)}, u32[]{:S(2)}, u32[]{:S(2)}) collective-permute-start(bf16[4,1024]{1,0:T(4,128)(2,1)S(1)} %slice.8), channel_id=1, source_target_pairs={{0,1},{2,3},{4,5},{6,7},{8,9},{10,11},{12,13},{14,15},{16,17},{18,... | collective-permute-start | bytes 24584
Sparse Core Ops, SparseCore 0:
  72.0 19.8 all-reduce.4
where the time goes:
time: 150 us
  blocking collectives  67.7 us (45%)
  matrix products  42.1 us (28%)
  waiting for transfers between devices  19.5 us (13%)
  between operations  14.1 us (9%)
  other arithmetic  2.64 us (2%)
  starting transfers between devices  2.26 us (2%)
  local copies, waits for them, and re-layouts  1.65 us (1%)
    all_gather x1, blocking collectives, shards(): lax.all_gather(tokens, 'mp', axis=0, tiled=True)  32.7 us
    all_gather x1, blocking collectives, shards(): lax.all_gather(activation, 'mp', axis=2, tiled=True)  32.1 us
    unnamed x3, waiting for transfers between devices  19.5 us
    dot_general x1, matrix products, projector(): jnp.einsum('td,dbf->tbf', piece, gate_part, preferred_element_type=jnp.fl...  15.7 us
    dot_general x1, matrix products, projector(): jnp.einsum('td,dbf->tbf', piece, up_part, preferred_element_type=jnp.floa...  15.7 us
    dot_general x1, matrix products, down_adder(): jnp.einsum('tbn,bnd->td', piece, weights, preferred_element_type=jnp.floa...  10.7 us
  transfers between devices with their start and end apart: 2, of which 2 were waited for; matrix products, arithmetic and copies ran while one was open for 0% of the time, Pallas kernels for 0%

commit v1 on v0

--- a/solution.py
+++ b/solution.py
@@ -1,7 +1,253 @@
+import functools
+
 import jax
 import jax.numpy as jnp
 from jax import lax
+from jax.experimental import pallas as pl
+from jax.experimental.pallas import tpu as pltpu
 from jax.sharding import PartitionSpec as P
+
+MESH = pl.DeviceIdType.MESH
+ROWS = 512
+SLOTS = 5
+VMEM_BYTES = 60 * 2**20
+
+
+def kernel(
+    n, cuts, x_ref, g_ref, u_ref, d_ref, o_ref,
+    wbuf, dbuf, tok, xs, xe, acc, part, act, oacc, obuf, orecv,
+    wsem, dsem, tsend, trecv, psend, precv, asend, arecv, osem,
+):
+    me = lax.axis_index("mp")
+    half = lax.axis_index("hidden")
+    other = 1 - half
+    rows, width = x_ref.shape
+    total, cols = act.shape[1:]
+    steps = width // ROWS
+
+    def peer(s):
+        return lax.rem(me + s, n)
+
+    def weight_copies(c, k, slot):
+        f0, fc = cuts[c]
+        start = pl.multiple_of(k * ROWS, ROWS)
+        return [
+            pltpu.make_async_copy(
+                ref.at[pl.ds(start, ROWS), :, pl.ds(f0, fc)],
+                wbuf.at[slot, i, :, :, pl.ds(0, fc)],
+                wsem.at[slot, i],
+            )
+            for i, ref in enumerate((g_ref, u_ref))
+        ]
+
+    def weight_start(c, k):
+        for copy in weight_copies(c, k, lax.rem(c * steps + k, SLOTS)):
+            copy.start()
+
+    def down_copy(c, s):
+        f0, fc = cuts[c]
+        p = peer(s)
+        window = pl.ds(pl.multiple_of(p * cols + f0, 128), fc)
+        return pltpu.make_async_copy(d_ref.at[0, window], dbuf.at[window], dsem.at[c, s])
+
+    for k in range(SLOTS):
+        weight_start(0, k)
+
+    barrier = pltpu.get_barrier_semaphore()
+    for s in range(1, n):
+        pl.semaphore_signal(barrier, inc=1, device_id={"mp": peer(s)}, device_id_type=MESH)
+    pl.semaphore_signal(barrier, inc=1, device_id={"hidden": other}, device_id_type=MESH)
+    pl.semaphore_wait(barrier, n)
+
+    def token_copy(s, slot):
+        return pltpu.make_async_remote_copy(
+            src_ref=x_ref, dst_ref=tok.at[slot], send_sem=tsend.at[s], recv_sem=trecv.at[slot],
+            device_id={"mp": peer(s)}, device_id_type=MESH,
+        )
+
+    for s in range(1, n):
+        token_copy(s, me).start()
+    tok[me] = x_ref[...]
+    for s in range(1, n):
+        token_copy(s, peer(s)).wait_recv()
+    for p in range(n):
+        xs[pl.ds(p * rows, rows), :] = tok[p].astype(jnp.float32)
+
+    place = lax.broadcasted_iota(jnp.int32, (128, 512), 0)
+    spot = lax.broadcasted_iota(jnp.int32, (128, 512), 1)
+    bank = spot // 256
+    spread = jnp.where(2 * place + bank == spot - 256 * bank, 1.0, 0.0).astype(jnp.bfloat16)
+    for j in range(width // 128):
+        both = jnp.dot(
+            xs[:, j * 128 : (j + 1) * 128].astype(jnp.bfloat16), spread,
+            preferred_element_type=jnp.float32,
+        )
+        both = jnp.concatenate([both[:, :256], both[:, 256:]], axis=0)
+        xe[:, j * 256 : (j + 1) * 256] = both.astype(jnp.bfloat16)
+
+    def part_copy(c):
+        f0, fc = cuts[c]
+        return pltpu.make_async_remote_copy(
+            src_ref=acc.at[:, other, :, pl.ds(f0, fc)], dst_ref=part.at[:, :, pl.ds(f0, fc)],
+            send_sem=psend.at[c], recv_sem=precv.at[c],
+            device_id={"hidden": other}, device_id_type=MESH,
+        )
+
+    def act_copy(c, s, slot):
+        f0, fc = cuts[c]
+        ref = act.at[slot, :, pl.ds(f0, fc)]
+        return pltpu.make_async_remote_copy(
+            src_ref=ref, dst_ref=ref, send_sem=asend.at[c, s], recv_sem=arecv.at[c, slot],
+            device_id={"mp": peer(s)}, device_id_type=MESH,
+        )
+
+    def activate(c):
+        f0, fc = cuts[c]
+        part_copy(c).wait_recv()
+        window = pl.ds(f0, fc)
+        gate = acc[0, half, :, window] + part[0, :, window]
+        up = acc[1, half, :, window] + part[1, :, window]
+        act[me, :, window] = (gate / (1.0 + jnp.exp(-gate)) * up).astype(jnp.bfloat16)
+        for s in range(1, n):
+            act_copy(c, s, me).start()
+
+    last = len(cuts) - 1
+    for c, (f0, fc) in enumerate(cuts):
+        window = pl.ds(f0, fc)
+        acc[:, :, :, window] = jnp.zeros((2, 2, total, fc), jnp.float32)
+
+        def step(k, carry, c=c, fc=fc, window=window):
+            slot = lax.rem(c * steps + k, SLOTS)
+            x = xe[:, pl.ds(pl.multiple_of(k * 2 * ROWS, 2 * ROWS), 2 * ROWS)]
+            for i, copy in enumerate(weight_copies(c, k, slot)):
+                copy.wait()
+                w = wbuf[slot, i, :, :, pl.ds(0, fc)].reshape(2 * ROWS, fc)
+                sums = jnp.dot(x, w, preferred_element_type=jnp.float32)
+                acc[i, :, :, window] += sums.reshape(2, total, fc)
+            ahead = k + SLOTS
+
+            @pl.when(ahead < steps)
+            def _():
+                weight_start(c, ahead)
+
+            if c < last:
+
+                @pl.when(ahead >= steps)
+                def _():
+                    weight_start(c + 1, ahead - steps)
+
+            else:
+                for j in range(n // 2):
+
+                    @pl.when(ahead - steps == j)
+                    def _():
+                        down_copy(0, 2 * j).start()
+                        down_copy(0, 2 * j + 1).start()
+
+            if c > 0:
+
+                @pl.when(k == 1)
+                def _():
+                    activate(c - 1)
+
+            return carry
+
+        lax.fori_loop(0, steps, step, 0)
+        part_copy(c).start()
+
+    for c in range(1, len(cuts)):
+        for s in range(n):
+            down_copy(c, s).start()
+
+    oacc[...] = jnp.zeros_like(oacc)
+
+    def down(c, s):
+        f0, fc = cuts[c]
+        p = peer(s)
+        if s > 0:
+            act_copy(c, s, p).wait_recv()
+        down_copy(c, s).wait()
+        oacc[...] += jnp.dot(
+            act[p, :, pl.ds(f0, fc)], dbuf[pl.ds(pl.multiple_of(p * cols + f0, 128), fc), :],
+            preferred_element_type=jnp.float32,
+        )
+
+    for c in range(last):
+        for s in range(n):
+            if c == 0 and s == 3:
+                activate(last)
+            down(c, s)
+    for s in range(n):
+        down(last, s)
+
+    own = total // 2
+    obuf[0] = oacc[:own, :]
+    obuf[1] = oacc[own:, :]
+    swap = pltpu.make_async_remote_copy(
+        src_ref=obuf.at[other], dst_ref=orecv, send_sem=osem.at[0], recv_sem=osem.at[1],
+        device_id={"hidden": other}, device_id_type=MESH,
+    )
+    swap.start()
+    swap.wait_recv()
+    o_ref[...] = (obuf[half] + orecv[...]).astype(jnp.bfloat16)
+
+    swap.wait_send()
+    for s in range(1, n):
+        token_copy(s, me).wait_send()
+    for c in range(len(cuts)):
+        part_copy(c).wait_send()
+        for s in range(1, n):
+            act_copy(c, s, me).wait_send()
+
+
+def fused(n, tokens, gate_weight, up_weight, down_weight):
+    rows, width = tokens.shape
+    cols = gate_weight.shape[2]
+    model = down_weight.shape[2]
+    total = n * rows
+    blocks = cols // 128
+    first = (blocks + 1) // 2 * 128
+    cuts = ((0, first), (first, cols - first))
+    vmem, dma = pltpu.VMEM, pltpu.SemaphoreType.DMA
+    in_vmem = pl.BlockSpec(memory_space=pltpu.VMEM)
+    in_hbm = pl.BlockSpec(memory_space=pl.ANY)
+    f32, bf16 = jnp.float32, jnp.bfloat16
+    weights = gate_weight.size + up_weight.size + down_weight.size
+    return pl.pallas_call(
+        functools.partial(kernel, n, cuts),
+        out_shape=jax.ShapeDtypeStruct((total // 2, model), bf16),
+        in_specs=[in_vmem, in_hbm, in_hbm, in_hbm],
+        out_specs=in_vmem,
+        scratch_shapes=[
+            vmem((SLOTS, 2, ROWS, 2, first), bf16),
+            vmem((n * cols, model), bf16),
+            vmem((n, rows, width), bf16),
+            vmem((total, width), f32),
+            vmem((2 * total, 2 * width), bf16),
+            vmem((2, 2, total, cols), f32),
+            vmem((2, total, cols), f32),
+            vmem((n, total, cols), bf16),
+            vmem((total, model), f32),
+            vmem((2, total // 2, model), f32),
+            vmem((total // 2, model), f32),
+            dma((SLOTS, 2)),
+            dma((2, n)),
+            dma((n,)),
+            dma((n,)),
+            dma((2,)),
+            dma((2,)),
+            dma((2, n)),
+            dma((2, n)),
+            dma((2,)),
+        ],
+        compiler_params=pltpu.CompilerParams(
+            collective_id=0, has_side_effects=True, vmem_limit_bytes=VMEM_BYTES
+        ),
+        cost_estimate=pl.CostEstimate(
+            flops=2 * total * weights, bytes_accessed=2 * weights,
+            transcendentals=total * cols,
+        ),
+    )(tokens, gate_weight, up_weight, down_weight)
 
 
 def projector(gate_part, up_part, piece):
@@ -14,7 +260,7 @@
     return jnp.einsum("tbn,bnd->td", piece, weights, preferred_element_type=jnp.float32)
 
 
-def shards(tokens, gate_weight, up_weight, down_weight):
+def plain(tokens, gate_weight, up_weight, down_weight):
     partial_sums = projector(
         gate_weight, up_weight, lax.all_gather(tokens, "mp", axis=0, tiled=True)
     )
@@ -25,7 +271,33 @@
     return mixed.astype(jnp.bfloat16)
 
 
+def fits(n, tokens, gate_weight, down_weight):
+    rows, width = tokens.shape
+    banks, cols = gate_weight.shape[1:]
+    total = n * rows
+    return (
+        banks == 2
+        and n % 2 == 0
+        and n >= 4
+        and total % 8 == 0
+        and total <= 64
+        and cols % 128 == 0
+        and cols >= 256
+        and down_weight.shape[2] % 128 == 0
+        and width % ROWS == 0
+        and width // ROWS >= SLOTS >= n // 2
+        and SLOTS * ROWS * 8 * (cols + 128) // 2 + down_weight.size * 2 < 52 * 2**20
+    )
+
+
 def solution(mesh):
+    n = mesh.shape["mp"]
+
+    def shards(tokens, gate_weight, up_weight, down_weight):
+        if mesh.shape["hidden"] == 2 and fits(n, tokens, gate_weight, down_weight):
+            return fused(n, tokens, gate_weight, up_weight, down_weight)
+        return plain(tokens, gate_weight, up_weight, down_weight)
+
     in_specs = (
         P(("groups", "mp"), "hidden"),
         P("hidden", None, "mp"),

time: 150 us -> 44 us (0.29)
  blocking collectives: 67.7 us -> 0 us
  Pallas kernels: 0 us -> 42.3 us
  matrix products: 42.1 us -> 0 us
  waiting for transfers between devices: 19.5 us -> 0 us
  between operations: 14.1 us -> 0.01 us
  other arithmetic: 2.64 us -> 0 us
  starting transfers between devices: 2.26 us -> 0 us
    all_gather x2 -> x0, blocking collectives: 64.8 us -> none  [the longest x1 32.7 us: shards(): lax.all_gather(tokens, 'mp', axis=0, tiled=True)]
    pallas_call x0 -> x1, Pallas kernels: none -> 42.3 us  [fused(): pl.pallas_call(functools.partial(kernel, n, cuts), out_shape=jax.ShapeDty...]
    dot_general x3 -> x0, matrix products: 42.1 us -> none  [the longest x1 15.7 us: projector(): jnp.einsum('td,dbf->tbf', piece, gate_part, preferred_element_type=jnp.fl...]
    unnamed x3 -> x0, waiting for transfers between devices: 19.5 us -> none
    unnamed x1 -> x0, blocking collectives: 2.96 us -> none
    unnamed x2 -> x0, starting transfers between devices: 2.26 us -> none
    convert_element_type x1 -> x0, other arithmetic: 1.73 us -> none  [shards(): activation = (jax.nn.silu(summed[0]) * summed[1]).astype(jnp.bfloat16)]
  transfers between devices with their start and end apart: 2 -> 0, of which waited for: 2 -> 0; matrix products, arithmetic and copies ran while one was open for 0% -> 0% of each run, Pallas kernels for 0% -> 0%
where the time goes in v1:
time: 44 us; the launch traced here: 43.7 us
  Pallas kernels  42.3 us (96%)
  local copies, waits for them, and re-layouts  1.38 us (3%)
    pallas_call x1, Pallas kernels, fused(): pl.pallas_call(functools.partial(kernel, n, cuts), out_shape=jax.ShapeDty...  42.3 us
    unnamed x1, local copies, waits for them, and re-layouts  1.38 us

profile of v1, /device:TPU:0, one launch (start us, length us, event | category | flops | bytes accessed | tf_op | source)
XLA Modules:
  0.0 43.7 jit_solution(6070725048874892866)
XLA Ops:
  0.0 42.3 %shard_map.46 = bf16[12,1024]{1,0:T(8,128)(2,1)} custom-call(bf16[3,4096]{1,0:T(4,128)(2,1)} %x_ref.1, bf16[4096,2,1664]{2,1,0:T(2,128)(2,1)} %g_ref.1, bf16[4096,2,1664]{2,1,0:T(2,128)(2,1)} %u_ref.1, bf16[1,13312,1024]{2,1,0:T(8,128)(2,1)} %d_ref.1), custom_call_target="tpu_custom_call" | custom-call | flops 1962934272 | bytes 81788928 | tf_op jit(solution)/shard_map/pallas_call | solution.py:216
  42.3 1.4 %copy.6 = bf16[12,1024]{1,0:T(8,128)(2,1)} copy(bf16[12,1024]{1,0:T(8,128)(2,1)} %shard_map.46) | data formatting | bytes 49152

commit v2 on v1

--- a/solution.py
+++ b/solution.py
@@ -25,8 +25,50 @@
     total, cols = act.shape[1:]
     steps = width // ROWS
 
-    def peer(s):
-        return lax.rem(me + s, n)
+    hops = n // 2
+    beside = me + 1 - 2 * lax.rem(me, 2)
+
+    def along(s):
+        return lax.rem(me + 2 * s, n)
+
+    def owner(s):
+        if s <= 1:
+            return (me, beside)[s]
+        return along(s - 1) if s <= hops else lax.rem(beside + 2 * (s - hops), n)
+
+    def direct(ref, ssem, rsem, j):
+        return pltpu.make_async_remote_copy(
+            src_ref=ref(me), dst_ref=ref(me), send_sem=ssem(j), recv_sem=rsem(me),
+            device_id={"mp": along(j) if j else beside}, device_id_type=MESH,
+        )
+
+    def onward(ref, ssem, rsem, j):
+        slot = along(j)
+        return pltpu.make_async_remote_copy(
+            src_ref=ref(slot), dst_ref=ref(slot), send_sem=ssem(hops + j), recv_sem=rsem(slot),
+            device_id={"mp": beside}, device_id_type=MESH,
+        )
+
+    def arrived(ref, ssem, rsem, slot):
+        pltpu.make_async_remote_copy(
+            src_ref=ref(slot), dst_ref=ref(slot), send_sem=ssem(0), recv_sem=rsem(slot),
+            device_id={"mp": beside}, device_id_type=MESH,
+        ).wait_recv()
+
+    def send(*gather):
+        for j in (*range(1, hops), 0):
+            direct(*gather, j).start()
+
+    def pass_on(*gather):
+        for j in range(1, hops):
+            arrived(*gather, along(j))
+            onward(*gather, j).start()
+
+    def sent(*gather):
+        for j in range(hops):
+            direct(*gather, j).wait_send()
+        for j in range(1, hops):
+            onward(*gather, j).wait_send()
 
     def weight_copies(c, k, slot):
         f0, fc = cuts[c]
@@ -46,7 +88,7 @@
 
     def down_copy(c, s):
         f0, fc = cuts[c]
-        p = peer(s)
+        p = owner(s)
         window = pl.ds(pl.multiple_of(p * cols + f0, 128), fc)
         return pltpu.make_async_copy(d_ref.at[0, window], dbuf.at[window], dsem.at[c, s])
 
@@ -54,36 +96,47 @@
         weight_start(0, k)
 
     barrier = pltpu.get_barrier_semaphore()
+    def peer(s):
+        return lax.rem(me + s, n)
+
     for s in range(1, n):
         pl.semaphore_signal(barrier, inc=1, device_id={"mp": peer(s)}, device_id_type=MESH)
     pl.semaphore_signal(barrier, inc=1, device_id={"hidden": other}, device_id_type=MESH)
     pl.semaphore_wait(barrier, n)
 
-    def token_copy(s, slot):
+    span = 2 * ROWS
+
+    def token_copy(t, s, slot):
+        window = pl.ds(pl.multiple_of(t * span, span), span)
         return pltpu.make_async_remote_copy(
-            src_ref=x_ref, dst_ref=tok.at[slot], send_sem=tsend.at[s], recv_sem=trecv.at[slot],
+            src_ref=x_ref.at[:, window], dst_ref=tok.at[slot, :, window],
+            send_sem=tsend.at[t, s], recv_sem=trecv.at[t, slot],
             device_id={"mp": peer(s)}, device_id_type=MESH,
         )
 
-    for s in range(1, n):
-        token_copy(s, me).start()
+    for t in range(steps // 2):
+        for s in range(1, n):
+            token_copy(t, s, me).start()
     tok[me] = x_ref[...]
-    for s in range(1, n):
-        token_copy(s, peer(s)).wait_recv()
-    for p in range(n):
-        xs[pl.ds(p * rows, rows), :] = tok[p].astype(jnp.float32)
-
-    place = lax.broadcasted_iota(jnp.int32, (128, 512), 0)
-    spot = lax.broadcasted_iota(jnp.int32, (128, 512), 1)
-    bank = spot // 256
-    spread = jnp.where(2 * place + bank == spot - 256 * bank, 1.0, 0.0).astype(jnp.bfloat16)
-    for j in range(width // 128):
-        both = jnp.dot(
-            xs[:, j * 128 : (j + 1) * 128].astype(jnp.bfloat16), spread,
-            preferred_element_type=jnp.float32,
-        )
-        both = jnp.concatenate([both[:, :256], both[:, 256:]], axis=0)
-        xe[:, j * 256 : (j + 1) * 256] = both.astype(jnp.bfloat16)
+
+    def prepare(t):
+        for s in range(1, n):
+            token_copy(t, s, peer(s)).wait_recv()
+        for p in range(n):
+            window = pl.ds(pl.multiple_of(t * span, span), span)
+            xs[pl.ds(p * rows, rows), :] = tok[p, :, window].astype(jnp.float32)
+        place = lax.broadcasted_iota(jnp.int32, (128, 512), 0)
+        spot = lax.broadcasted_iota(jnp.int32, (128, 512), 1)
+        bank = spot // 256
+        spread = jnp.where(2 * place + bank == spot - 256 * bank, 1.0, 0.0).astype(jnp.bfloat16)
+        for j in range(span // 128):
+            both = jnp.dot(
+                xs[:, j * 128 : (j + 1) * 128].astype(jnp.bfloat16), spread,
+                preferred_element_type=jnp.float32,
+            )
+            both = jnp.concatenate([both[:, :256], both[:, 256:]], axis=0)
+            start = pl.multiple_of(t * 2 * span + j * 256, 256)
+            xe[:, pl.ds(start, 256)] = both.astype(jnp.bfloat16)
 
     def part_copy(c):
         f0, fc = cuts[c]
@@ -93,12 +146,12 @@
             device_id={"hidden": other}, device_id_type=MESH,
         )
 
-    def act_copy(c, s, slot):
-        f0, fc = cuts[c]
-        ref = act.at[slot, :, pl.ds(f0, fc)]
-        return pltpu.make_async_remote_copy(
-            src_ref=ref, dst_ref=ref, send_sem=asend.at[c, s], recv_sem=arecv.at[c, slot],
-            device_id={"mp": peer(s)}, device_id_type=MESH,
+    def acts(c):
+        f0, fc = cuts[c]
+        return (
+            lambda slot: act.at[slot, :, pl.ds(f0, fc)],
+            lambda j: asend.at[c, j],
+            lambda slot: arecv.at[c, slot],
         )
 
     def activate(c):
@@ -108,22 +161,43 @@
         gate = acc[0, half, :, window] + part[0, :, window]
         up = acc[1, half, :, window] + part[1, :, window]
         act[me, :, window] = (gate / (1.0 + jnp.exp(-gate)) * up).astype(jnp.bfloat16)
-        for s in range(1, n):
-            act_copy(c, s, me).start()
-
+        send(*acts(c))
+
+    pieces = [(c, s) for c in range(len(cuts)) for s in range(n)]
     last = len(cuts) - 1
     for c, (f0, fc) in enumerate(cuts):
         window = pl.ds(f0, fc)
         acc[:, :, :, window] = jnp.zeros((2, 2, total, fc), jnp.float32)
 
-        def step(k, carry, c=c, fc=fc, window=window):
+        def step(k, carry, c=c, f0=f0, fc=fc):
+            if c == 0:
+
+                @pl.when(lax.rem(k, 2) == 0)
+                def _():
+                    prepare(k // 2)
+
             slot = lax.rem(c * steps + k, SLOTS)
             x = xe[:, pl.ds(pl.multiple_of(k * 2 * ROWS, 2 * ROWS), 2 * ROWS)]
-            for i, copy in enumerate(weight_copies(c, k, slot)):
-                copy.wait()
-                w = wbuf[slot, i, :, :, pl.ds(0, fc)].reshape(2 * ROWS, fc)
+            copies = weight_copies(c, k, slot)
+
+            def block(i, at, wide):
+                return wbuf[slot, i, :, :, pl.ds(at, wide)].reshape(2 * ROWS, wide)
+
+            def add(i, at, sums):
+                wide = sums.shape[1]
+                acc[i, :, :, pl.ds(f0 + at, wide)] += sums.reshape(2, total, wide)
+
+            rest = fc % 256
+            for i in range(2):
+                copies[i].wait()
+                for at in range(0, fc - rest, 512):
+                    wide = min(512, fc - rest - at)
+                    add(i, at, jnp.dot(x, block(i, at, wide), preferred_element_type=jnp.float32))
+            if rest:
+                w = jnp.concatenate([block(0, fc - rest, rest), block(1, fc - rest, rest)], axis=1)
                 sums = jnp.dot(x, w, preferred_element_type=jnp.float32)
-                acc[i, :, :, window] += sums.reshape(2, total, fc)
+                add(0, fc - rest, sums[:, :rest])
+                add(1, fc - rest, sums[:, rest:])
             ahead = k + SLOTS
 
             @pl.when(ahead < steps)
@@ -137,12 +211,12 @@
                     weight_start(c + 1, ahead - steps)
 
             else:
-                for j in range(n // 2):
+                for j in range(SLOTS):
 
                     @pl.when(ahead - steps == j)
-                    def _():
-                        down_copy(0, 2 * j).start()
-                        down_copy(0, 2 * j + 1).start()
+                    def _(j=j):
+                        for piece in pieces[2 * j : 2 * j + 2]:
+                            down_copy(*piece).start()
 
             if c > 0:
 
@@ -150,35 +224,37 @@
                 def _():
                     activate(c - 1)
 
+                @pl.when(k == 5)
+                def _():
+                    pass_on(*acts(c - 1))
+
             return carry
 
         lax.fori_loop(0, steps, step, 0)
         part_copy(c).start()
 
-    for c in range(1, len(cuts)):
-        for s in range(n):
-            down_copy(c, s).start()
+    for piece in pieces[2 * SLOTS :]:
+        down_copy(*piece).start()
 
     oacc[...] = jnp.zeros_like(oacc)
 
     def down(c, s):
         f0, fc = cuts[c]
-        p = peer(s)
-        if s > 0:
-            act_copy(c, s, p).wait_recv()
+        p = owner(s)
+        if s == 1 or s > hops:
+            arrived(*acts(c), p)
         down_copy(c, s).wait()
         oacc[...] += jnp.dot(
             act[p, :, pl.ds(f0, fc)], dbuf[pl.ds(pl.multiple_of(p * cols + f0, 128), fc), :],
             preferred_element_type=jnp.float32,
         )
 
-    for c in range(last):
-        for s in range(n):
-            if c == 0 and s == 3:
-                activate(last)
-            down(c, s)
-    for s in range(n):
-        down(last, s)
+    for c, s in pieces:
+        if (c, s) == (0, 2):
+            activate(last)
+        if (c, s) == (last, 0):
+            pass_on(*acts(last))
+        down(c, s)
 
     own = total // 2
     obuf[0] = oacc[:own, :]
@@ -189,15 +265,15 @@
     )
     swap.start()
     swap.wait_recv()
-    o_ref[...] = (obuf[half] + orecv[...]).astype(jnp.bfloat16)
+    o_ref[...] = obuf[half] + orecv[...]
 
     swap.wait_send()
-    for s in range(1, n):
-        token_copy(s, me).wait_send()
+    for t in range(steps // 2):
+        for s in range(1, n):
+            token_copy(t, s, me).wait_send()
     for c in range(len(cuts)):
         part_copy(c).wait_send()
-        for s in range(1, n):
-            act_copy(c, s, me).wait_send()
+        sent(*acts(c))
 
 
 def fused(n, tokens, gate_weight, up_weight, down_weight):
@@ -205,9 +281,10 @@
     cols = gate_weight.shape[2]
     model = down_weight.shape[2]
     total = n * rows
-    blocks = cols // 128
-    first = (blocks + 1) // 2 * 128
+    first = (cols // 128 * 13 // 20 + 1) // 2 * 256
     cuts = ((0, first), (first, cols - first))
+    count = len(cuts)
+    widest = max(fc for _, fc in cuts) // 128 // 2 * 256 + 128
     vmem, dma = pltpu.VMEM, pltpu.SemaphoreType.DMA
     in_vmem = pl.BlockSpec(memory_space=pltpu.VMEM)
     in_hbm = pl.BlockSpec(memory_space=pl.ANY)
@@ -215,14 +292,14 @@
     weights = gate_weight.size + up_weight.size + down_weight.size
     return pl.pallas_call(
         functools.partial(kernel, n, cuts),
-        out_shape=jax.ShapeDtypeStruct((total // 2, model), bf16),
+        out_shape=jax.ShapeDtypeStruct((total // 2, model), f32),
         in_specs=[in_vmem, in_hbm, in_hbm, in_hbm],
         out_specs=in_vmem,
         scratch_shapes=[
-            vmem((SLOTS, 2, ROWS, 2, first), bf16),
+            vmem((SLOTS, 2, ROWS, 2, widest), bf16),
             vmem((n * cols, model), bf16),
             vmem((n, rows, width), bf16),
-            vmem((total, width), f32),
+            vmem((total, 2 * ROWS), f32),
             vmem((2 * total, 2 * width), bf16),
             vmem((2, 2, total, cols), f32),
             vmem((2, total, cols), f32),
@@ -231,13 +308,13 @@
             vmem((2, total // 2, model), f32),
             vmem((total // 2, model), f32),
             dma((SLOTS, 2)),
-            dma((2, n)),
-            dma((n,)),
-            dma((n,)),
-            dma((2,)),
-            dma((2,)),
-            dma((2, n)),
-            dma((2, n)),
+            dma((count, n)),
+            dma((width // ROWS // 2, n)),
+            dma((width // ROWS // 2, n)),
+            dma((count,)),
+            dma((count,)),
+            dma((count, n)),
+            dma((count, n)),
             dma((2,)),
         ],
         compiler_params=pltpu.CompilerParams(
@@ -247,7 +324,7 @@
             flops=2 * total * weights, bytes_accessed=2 * weights,
             transcendentals=total * cols,
         ),
-    )(tokens, gate_weight, up_weight, down_weight)
+    )(tokens, gate_weight, up_weight, down_weight).astype(bf16)
 
 
 def projector(gate_part, up_part, piece):
@@ -282,11 +359,12 @@
         and total % 8 == 0
         and total <= 64
         and cols % 128 == 0
-        and cols >= 256
+        and cols >= 640
         and down_weight.shape[2] % 128 == 0
-        and width % ROWS == 0
-        and width // ROWS >= SLOTS >= n // 2
-        and SLOTS * ROWS * 8 * (cols + 128) // 2 + down_weight.size * 2 < 52 * 2**20
+        and width % (2 * ROWS) == 0
+        and width // ROWS >= SLOTS
+        and width // ROWS > 5
+        and SLOTS * ROWS * 8 * (cols * 13 // 20 + 256) + down_weight.size * 2 < 53 * 2**20
     )
 
 

time: 44 us -> 43.4 us (0.986)
  other arithmetic: 0 us -> 1.46 us
  local copies, waits for them, and re-layouts: 1.38 us -> 0 us
  Pallas kernels: 42.3 us -> 41.7 us
    convert_element_type x0 -> x1, other arithmetic: none -> 1.46 us  [fused(): return pl.pallas_call(functools.partial(kernel, n, cuts), out_shape=jax.S...]
    unnamed x1 -> x0, local copies, waits for them, and re-layouts: 1.38 us -> none
    pallas_call x1, Pallas kernels: 42.3 us -> 41.7 us  [fused(): pl.pallas_call(functools.partial(kernel, n, cuts), out_shape=jax.ShapeDty...]
where the time goes in v2:
time: 43.4 us; the launch traced here: 43.2 us
  Pallas kernels  41.7 us (96%)
  other arithmetic  1.46 us (3%)
    pallas_call x1, Pallas kernels, fused(): pl.pallas_call(functools.partial(kernel, n, cuts), out_shape=jax.ShapeDty...  41.7 us
    convert_element_type x1, other arithmetic, fused(): return pl.pallas_call(functools.partial(kernel, n, cuts), out_shape=jax.S...  1.46 us

profile of v2, /device:TPU:0, one launch (start us, length us, event | category | flops | bytes accessed | tf_op | source)
XLA Modules:
  0.0 43.2 jit_solution(13067823105644258225)
XLA Ops:
  0.0 41.7 %shard_map.46 = f32[12,1024]{1,0:T(8,128)} custom-call(bf16[3,4096]{1,0:T(4,128)(2,1)} %x_ref.1, bf16[4096,2,1664]{2,1,0:T(2,128)(2,1)} %g_ref.1, bf16[4096,2,1664]{2,1,0:T(2,128)(2,1)} %u_ref.1, bf16[1,13312,1024]{2,1,0:T(8,128)(2,1)} %d_ref.1), custom_call_target="tpu_custom_call" | custom-call | flops 1962934272 | bytes 81788928 | tf_op jit(solution)/shard_map/pallas_call | solution.py:293
  41.7 1.5 %convert_element_type.3 = bf16[12,1024]{1,0:T(8,128)(2,1)} convert(f32[12,1024]{1,0:T(8,128)} %shard_map.46) | non-fusion elementwise | flops 12288 | bytes 73728 | tf_op jit(solution)/shard_map/convert_element_type | solution.py:327
